TPU v7x, 128 devices: a whole 4x4x4 slice. The times are simulated.
128 devices in a mesh: chain: 32 (over x_hi, z, y), tm: 4 (over x_lo, core).
Axes of the slice: x: 4 (x_hi: 2, x_lo: 2; x = x_hi * 2 + x_lo), y: 4, z: 4, core: 2. Of those that a mesh axis runs over, the one named last changes fastest.
Arguments:
- traces: bfloat16 [2048, 128, 512], P('chain', 'tm'), may hold values from -6 to 6
Outputs:
- stack: float32 [2048, 2, 256, 256], P('chain', None, 'tm')
All inputs are finite; a program needn't handle non-finite values.
Results may differ from a plain program's by a relative error of at most 0.012.
Values may be sent and summed in bfloat16 or wider, within the bound.
A program may use at most 256 MiB of HBM per device.

v0:
```python
import math

import jax
import jax.numpy as jnp
from jax import lax
from jax.sharding import PartitionSpec as P

LAG = 256


def passed_along(block, axis, distance):
    devices = range(lax.axis_size(axis))
    route = [(i - distance, i) for i in devices if i - distance in devices]
    return lax.ppermute(block, axis, route)


def kernel_table(length, bins):
    samples = jnp.arange(length, dtype=jnp.int32)
    freqs = jnp.arange(bins, dtype=jnp.int32)
    phase_index = samples[:, None] * freqs[None, :] % length
    angles = 2.0 * math.pi / length * phase_index.astype(jnp.float32)
    window_taper = 0.5 - 0.5 * jnp.cos(2.0 * math.pi / length * samples.astype(jnp.float32))
    cosines = window_taper[:, None] * jnp.cos(angles)
    sines = -window_taper[:, None] * jnp.sin(angles)
    return jnp.concatenate([cosines, sines], axis=1).astype(jnp.bfloat16)


def whiten(traces_block, kernel):
    channels, windows, length = traces_block.shape
    bins = kernel.shape[1] // 2
    spectra = jnp.dot(
        traces_block.reshape(channels * windows, length), kernel, preferred_element_type=jnp.float32
    )
    real_part = spectra[:, :bins]
    imag_part = spectra[:, bins:]
    magnitude = jnp.sqrt(real_part * real_part + imag_part * imag_part)
    mean_level = jnp.mean(magnitude, axis=-1, keepdims=True)
    divisor = magnitude + 0.1 * (mean_level + 1e-06)
    merged = jnp.concatenate([real_part / divisor, imag_part / divisor], axis=1).astype(
        jnp.bfloat16
    )
    return jnp.transpose(merged.reshape(channels, windows, 2, bins), (0, 2, 1, 3))


def lag_band(matrix, lags):
    leading = matrix.shape[:-2]
    channels = matrix.shape[-2]
    columns = matrix.shape[-1]
    flattened = matrix.reshape(leading + (channels * columns,))
    pad_spec = [(0, 0)] * len(leading) + [(0, channels)]
    flattened = jnp.pad(flattened, pad_spec)
    return flattened.reshape(leading + (channels, columns + 1))[..., :lags]


def segment_stack(own, reach, lags, scale):
    own_real = own[:, 0]
    own_imag = own[:, 1]
    turned = jnp.stack([own_imag, -own_real], axis=1)
    left_rows = jnp.concatenate([own, turned], axis=0)
    products = jnp.einsum("apwf,jpwf->faj", left_rows, reach, preferred_element_type=jnp.float32)
    channels = own.shape[0]
    real_band = lag_band(products[:, :channels], lags)
    imag_band = lag_band(products[:, channels:], lags)
    stacked = jnp.stack([real_band, imag_band], axis=0)
    return (jnp.transpose(stacked, (2, 0, 1, 3)) * scale).astype(jnp.bfloat16)


def upper_blocks(block):
    reach_count = LAG // block.shape[0]
    pieces = [block]
    current = block
    for offset in range(reach_count):
        current = passed_along(current, "chain", -1)
        pieces.append(current)
    return pieces


def blocked_stack(own, pieces, lower, upper, scale):
    bins = own.shape[3]
    step_bins = math.gcd(128, bins)
    results = []
    for first_bin in range(0, bins, step_bins):
        last_bin = first_bin + step_bins
        reach = jnp.concatenate(
            [piece[:, :, lower:upper, first_bin:last_bin] for piece in pieces], axis=0
        )
        results.append(segment_stack(own[:, :, lower:upper, first_bin:last_bin], reach, LAG, scale))
    return jnp.concatenate(results, axis=2)


def per_device(traces):
    channels, windows, length = traces.shape
    bins = length // 2
    kernel = kernel_table(length, bins)
    whitened = whiten(traces, kernel)
    segments = lax.axis_size("tm")
    scale = 1.0 / math.sqrt(windows * segments)
    pieces = upper_blocks(whitened)
    hour = blocked_stack(whitened, pieces, 0, windows, scale)
    term = lax.optimization_barrier(hour).astype(jnp.float32)
    return lax.psum_scatter(
        term.astype(jnp.bfloat16), "tm", scatter_dimension=2, tiled=True
    ).astype(jnp.float32)


def solution(mesh):
    placed = (P("chain", "tm", None),)
    return jax.shard_map(
        per_device,
        mesh=mesh,
        in_specs=placed,
        out_specs=P("chain", None, "tm", None),
        check_vma=False,
    )
```

profile of v0, /device:TPU:1, one launch (start us, length us, event | category | flops | bytes accessed | tf_op | source)
XLA Modules:
  0.0 756.1 jit_solution(11945228156322293431)
XLA Ops:
  6.5 0.0 reduce-scatter.2.cloned.1.call-start
  6.6 2.3 multiply_convert_fusion
  9.0 1.3 convolution_bitcast_fusion.2
  10.3 0.8 fusion.27
  11.1 1.0 divide_convert_fusion.1
  12.1 0.2 pad_maximum_fusion.1
  12.3 2.5 copy.10
  14.8 2.5 convert_element_type.47
  17.4 0.5 copy.39
  17.9 1.3 collective-permute-start
  19.2 47.7 %collective-permute-done = bf16[64,2,32,256]{3,2,1,0:T(8,128)(2,1)S(1)} collective-permute-done((bf16[64,2,32,256]{3,2,1,0:T(8,128)(2,1)S(1)}, bf16[64,2,32,256]{3,2,1,0:T(8,128)(2,1)S(1)}, u32[]{:S(2)}, u32[]{:S(2)}) %collective-permute-start) | collective-permute-done | bytes 2097184 | tf_op jit(solution)/shard_map/ppermute | solution.py:14
  66.9 1.3 collective-permute-start.1
  68.1 46.3 %collective-permute-done.1 = bf16[64,2,32,256]{3,2,1,0:T(8,128)(2,1)S(1)} collective-permute-done((bf16[64,2,32,256]{3,2,1,0:T(8,128)(2,1)S(1)}, bf16[64,2,32,256]{3,2,1,0:T(8,128)(2,1)S(1)}, u32[]{:S(2)}, u32[]{:S(2)}) %collective-permute-start.1) | collective-permute-done | bytes 2097184 | tf_op jit(solution)/shard_map/ppermute | solution.py:14
  114.4 1.4 copy-done.4
  115.8 1.3 collective-permute-start.2
  117.1 45.4 %collective-permute-done.2 = bf16[64,2,32,256]{3,2,1,0:T(8,128)(2,1)} collective-permute-done((bf16[64,2,32,256]{3,2,1,0:T(8,128)(2,1)S(1)}, bf16[64,2,32,256]{3,2,1,0:T(8,128)(2,1)}, u32[]{:S(2)}, u32[]{:S(2)}) %collective-permute-start.2) | collective-permute-done | bytes 2097184 | tf_op jit(solution)/shard_map/ppermute | solution.py:14
  162.4 1.8 collective-permute-start.3
  164.2 6.5 copy.11
  170.7 4.5 fusion.30
  175.2 2.3 fusion.31
  177.5 1.6 fusion.35
  179.1 5.4 copy.30
  184.5 4.4 copy.34
  189.0 2.9 fusion.34
  191.9 5.5 copy.31
  197.4 4.4 copy.35
  201.8 2.9 fusion.33
  204.7 5.4 copy.32
  210.2 4.6 copy.36
  214.8 0.0 collective-permute-done.3
  214.8 2.9 fusion.32
  217.7 5.4 copy.33
  223.2 13.1 %concatenate.26 = bf16[320,2,32,128]{0,2,1,3:T(8,128)(2,1)} concatenate(bf16[64,2,32,128]{0,2,1,3:T(8,128)(2,1)} %get-tuple-element.15, bf16[64,2,32,128]{0,2,1,3:T(8,128)(2,1)} %copy.30, bf16[64,2,32,128]{0,2,1,3:T(8,128)(2,1)} %copy.31, bf16[64,2,32,128]{0,2,1,3:T(8,128)(2,1)} %copy.32, bf16[64,2,32,128]{0,2,1,3:T(8,128)(2,1)} %copy.33), dimensions={0} | concatenate | bytes 10485760 | tf_op jit(solution)/shard_map/concatenate | solution.py:84
  236.3 14.8 %convolution_bitcast_fusion.1 = f32[128,128,320]{1,2,0:T(8,128)} fusion(bf16[320,2,32,128]{0,2,1,3:T(8,128)(2,1)} %concatenate.26, bf16[64,1,32,128]{0,2,1,3:T(8,128)(2,1)} %get-tuple-element.14, bf16[64,1,32,128]{0,2,1,3:T(8,128)(2,1)} %get-tuple-element.11, bf16[64,2,32,128]{0,2,1,3:T(8,128)(2,1)} %get-tuple-element.15), kind=kOutput, calls=%fused_computation.6 | convolution fusion | flops 677380096 | bytes 28311552 | tf_op jit(solution)/shard_map/apwf,jpwf->faj/dot_general | solution.py:60
  251.1 30.6 %fusion.28 = (f32[128,64,320]{1,2,0:T(8,128)}, f32[128,64,320]{1,2,0:T(8,128)}) fusion(f32[128,128,320]{1,2,0:T(8,128)} %convolution_bitcast_fusion.1), kind=kLoop, calls=%fused_computation.52 | loop fusion | bytes 41943040 | tf_op jit(solution)/shard_map/slice | solution.py:62
  281.7 19.2 %copy.18 = f32[128,64,320]{0,2,1:T(8,128)} copy(f32[128,64,320]{1,2,0:T(8,128)} %get-tuple-element.6) | data formatting | bytes 20971520 | tf_op jit(solution)/shard_map/slice | solution.py:63
  300.9 8.9 %pad.14 = f32[128,20544]{0,1:T(8,128)} pad(f32[128,20480]{0,1:T(8,128)} %bitcast.42, f32[]{:T(128)} %constant.28.clone.1), padding=0_0x0_64 | pad | bytes 21004292 | tf_op jit(solution)/shard_map/jit(_pad)/pad | solution.py:51
  309.8 10.3 %reshape.54 = f32[128,64,321]{0,2,1:T(8,128)} reshape(f32[128,20544]{0,1:T(8,128)} %pad.14) | data formatting | bytes 21037056 | tf_op jit(solution)/shard_map/reshape | solution.py:52
  320.0 7.6 %slice_bitcast_fusion.2 = f32[1,128,64,256]{1,3,2,0:T(8,128)} fusion(f32[128,64,321]{0,2,1:T(8,128)} %reshape.54), kind=kLoop, calls=%fused_computation.11 | loop fusion | bytes 16777216 | tf_op jit(solution)/shard_map/stack | solution.py:64
  327.7 19.4 %copy.17 = f32[128,64,320]{0,2,1:T(8,128)} copy(f32[128,64,320]{1,2,0:T(8,128)} %get-tuple-element.5) | data formatting | bytes 20971520 | tf_op jit(solution)/shard_map/slice | solution.py:62
  347.0 8.9 %pad.13 = f32[128,20544]{0,1:T(8,128)} pad(f32[128,20480]{0,1:T(8,128)} %bitcast.43, f32[]{:T(128)} %constant.28.clone.1), padding=0_0x0_64 | pad | bytes 21004292 | tf_op jit(solution)/shard_map/jit(_pad)/pad | solution.py:51
  355.9 10.3 %reshape.52 = f32[128,64,321]{0,2,1:T(8,128)} reshape(f32[128,20544]{0,1:T(8,128)} %pad.13) | data formatting | bytes 21037056 | tf_op jit(solution)/shard_map/reshape | solution.py:52
  366.2 7.6 %slice_bitcast_fusion.3 = f32[1,128,64,256]{1,3,2,0:T(8,128)} fusion(f32[128,64,321]{0,2,1:T(8,128)} %reshape.52), kind=kLoop, calls=%fused_computation.12 | loop fusion | bytes 16777216 | tf_op jit(solution)/shard_map/stack | solution.py:64
  373.9 4.5 copy.37
  378.4 12.8 %concatenate.28 = bf16[320,2,32,128]{0,2,1,3:T(8,128)(2,1)} concatenate(bf16[64,2,32,128]{0,2,1,3:T(8,128)(2,1)S(1)} %get-tuple-element.16, bf16[64,2,32,128]{0,2,1,3:T(8,128)(2,1)} %copy.34, bf16[64,2,32,128]{0,2,1,3:T(8,128)(2,1)} %copy.35, bf16[64,2,32,128]{0,2,1,3:T(8,128)(2,1)} %copy.36, bf16[64,2,32,128]{0,2,1,3:T(8,128)(2,1)} %copy.37), dimensions={0} | concatenate | bytes 10485760 | tf_op jit(solution)/shard_map/concatenate | solution.py:84
  391.2 13.9 %convolution_bitcast_fusion = f32[128,128,320]{1,2,0:T(8,128)} fusion(bf16[320,2,32,128]{0,2,1,3:T(8,128)(2,1)} %concatenate.28, bf16[64,1,32,128]{0,2,1,3:T(8,128)(2,1)} %get-tuple-element.13, bf16[64,1,32,128]{0,2,1,3:T(8,128)(2,1)S(1)} %copy-done.3, bf16[64,2,32,128]{0,2,1,3:T(8,128)(2,1)S(1)} %get-tuple-element.16), kind=kOutput, calls=%fused_computation.5 | convolution fusion | flops 677380096 | bytes 28311552 | tf_op jit(solution)/shard_map/apwf,jpwf->faj/dot_general | solution.py:60
  405.0 30.6 %fusion.29 = (f32[128,64,320]{1,2,0:T(8,128)}, f32[128,64,320]{1,2,0:T(8,128)}) fusion(f32[128,128,320]{1,2,0:T(8,128)} %convolution_bitcast_fusion), kind=kLoop, calls=%fused_computation.53 | loop fusion | bytes 41943040 | tf_op jit(solution)/shard_map/slice | solution.py:62
  435.6 19.2 %copy.24 = f32[128,64,320]{0,2,1:T(8,128)} copy(f32[128,64,320]{1,2,0:T(8,128)} %get-tuple-element.8) | data formatting | bytes 20971520 | tf_op jit(solution)/shard_map/slice | solution.py:63
  454.8 8.9 %pad.16 = f32[128,20544]{0,1:T(8,128)} pad(f32[128,20480]{0,1:T(8,128)} %bitcast.44, f32[]{:T(128)} %constant.28.clone.1), padding=0_0x0_64 | pad | bytes 21004292 | tf_op jit(solution)/shard_map/jit(_pad)/pad | solution.py:51
  463.7 10.3 %reshape.58 = f32[128,64,321]{0,2,1:T(8,128)} reshape(f32[128,20544]{0,1:T(8,128)} %pad.16) | data formatting | bytes 21037056 | tf_op jit(solution)/shard_map/reshape | solution.py:52
  474.0 7.8 %slice_bitcast_fusion = f32[1,128,64,256]{1,3,2,0:T(8,128)} fusion(f32[128,64,321]{0,2,1:T(8,128)} %reshape.58), kind=kLoop, calls=%fused_computation.9 | loop fusion | bytes 16777216 | tf_op jit(solution)/shard_map/stack | solution.py:64
  481.7 19.4 %copy.23 = f32[128,64,320]{0,2,1:T(8,128)} copy(f32[128,64,320]{1,2,0:T(8,128)} %get-tuple-element.7) | data formatting | bytes 20971520 | tf_op jit(solution)/shard_map/slice | solution.py:62
  501.1 8.9 %pad.15 = f32[128,20544]{0,1:T(8,128)} pad(f32[128,20480]{0,1:T(8,128)} %bitcast.41, f32[]{:T(128)} %constant.28.clone.1), padding=0_0x0_64 | pad | bytes 21004292 | tf_op jit(solution)/shard_map/jit(_pad)/pad | solution.py:51
  510.0 10.3 %reshape.56 = f32[128,64,321]{0,2,1:T(8,128)} reshape(f32[128,20544]{0,1:T(8,128)} %pad.15) | data formatting | bytes 21037056 | tf_op jit(solution)/shard_map/reshape | solution.py:52
  520.4 4.1 slice_bitcast_fusion.1
  524.4 0.0 slice-start.1
  524.5 7.2 fusion.3
  531.7 4.5 fusion.2
  536.3 10.8 %pad_maximum_fusion = bf16[64,2,256,256]{2,3,0,1:T(8,128)(2,1)} fusion(bf16[64,2,128,256]{2,3,0,1:T(8,128)(2,1)} %fusion.2, bf16[64,2,128,256]{2,3,0,1:T(8,128)(2,1)S(1)} %fusion.3), kind=kLoop, calls=%fused_computation.4 | loop fusion | flops 33554432 | bytes 33554432 | tf_op jit(solution)/shard_map/concatenate | solution.py:88
  547.1 23.0 %copy.25 = bf16[64,2,256,256]{3,0,1,2:T(8,128)(2,1)} copy(bf16[64,2,256,256]{2,3,0,1:T(8,128)(2,1)} %pad_maximum_fusion) | data formatting | bytes 33554432 | tf_op jit(solution)/shard_map/optimization_barrier | solution.py:100
  570.1 0.0 reduce-scatter.2.cloned.1.call-update
  570.1 0.0 copy-start.1
  570.1 170.8 %reduce-scatter.2.cloned.1.call-done = bf16[64,2,64,256]{3,0,1,2:T(8,128)(2,1)} async-done(((bf16[64,2,256,256]{3,0,1,2:T(8,128)(2,1)}), bf16[64,2,64,256]{3,0,1,2:T(8,128)(2,1)}) %reduce-scatter.2.cloned.1.call-update) | async-done | bytes 4194320 | tf_op jit(solution)/shard_map/reduce_scatter | solution.py:101
  741.0 8.0 %copy.26 = f32[64,2,64,256]{3,2,1,0:T(8,128)} copy(bf16[64,2,64,256]{3,0,1,2:T(8,128)(2,1)} %reduce-scatter.2.cloned.1.call-done) | data formatting | bytes 12582912 | tf_op jit(solution)/shard_map/convert_element_type | solution.py:103
  (19 shorter events, 0.1 us)
Async XLA Ops:
  6.5 2.4 copy-start
  6.5 734.4 %reduce-scatter.2.cloned.1.call-start = ((), (), s32[]{:S(2)}) async-start(), calls=%async_computation.1 | async-start | bytes 20971520 | tf_op jit(solution)/shard_map/reduce_scatter | solution.py:101
  17.9 49.0 %collective-permute-start = (bf16[64,2,32,256]{3,2,1,0:T(8,128)(2,1)S(1)}, bf16[64,2,32,256]{3,2,1,0:T(8,128)(2,1)S(1)}, u32[]{:S(2)}, u32[]{:S(2)}) collective-permute-start(bf16[64,2,32,256]{3,2,1,0:T(8,128)(2,1)S(1)} %bitcast.49), channel_id=1, source_target_pairs={{4,0},{8,4},{12,8},{16,12},{20,16},{24,20},{28,24},{32,28},{36,32}... | collective-permute-start | bytes 6291464 | tf_op jit(solution)/shard_map/ppermute | solution.py:14
  66.9 95.6 %copy-start.5 = (bf16[64,2,32,256]{3,2,1,0:T(8,128)(2,1)}, bf16[64,2,32,256]{3,2,1,0:T(8,128)(2,1)S(1)}, u32[]{:S(2)}) copy-start(bf16[64,2,32,256]{3,2,1,0:T(8,128)(2,1)S(1)} %collective-permute-done) | copy-start | bytes 6291460
  66.9 47.5 %collective-permute-start.1 = (bf16[64,2,32,256]{3,2,1,0:T(8,128)(2,1)S(1)}, bf16[64,2,32,256]{3,2,1,0:T(8,128)(2,1)S(1)}, u32[]{:S(2)}, u32[]{:S(2)}) collective-permute-start(bf16[64,2,32,256]{3,2,1,0:T(8,128)(2,1)S(1)} %collective-permute-done), channel_id=1, source_target_pairs={{4,0},{8,4},{12,8},{16,12},{20,16},{24,20},{28,24},{32,28},{36,32}... | collective-permute-start | bytes 6291464 | tf_op jit(solution)/shard_map/ppermute | solution.py:14
  114.4 1.4 copy-start.4
  115.8 46.6 %collective-permute-start.2 = (bf16[64,2,32,256]{3,2,1,0:T(8,128)(2,1)S(1)}, bf16[64,2,32,256]{3,2,1,0:T(8,128)(2,1)}, u32[]{:S(2)}, u32[]{:S(2)}) collective-permute-start(bf16[64,2,32,256]{3,2,1,0:T(8,128)(2,1)S(1)} %collective-permute-done.1), channel_id=1, source_target_pairs={{4,0},{8,4},{12,8},{16,12},{20,16},{24,20},{28,24},{32,28},{36,32}... | collective-permute-start | bytes 6291464 | tf_op jit(solution)/shard_map/ppermute | solution.py:14
  162.4 52.4 %collective-permute-start.3 = (bf16[64,2,32,256]{3,2,1,0:T(8,128)(2,1)}, bf16[64,2,32,256]{3,2,1,0:T(8,128)(2,1)}, u32[]{:S(2)}, u32[]{:S(2)}) collective-permute-start(bf16[64,2,32,256]{3,2,1,0:T(8,128)(2,1)} %collective-permute-done.2), channel_id=1, source_target_pairs={{4,0},{8,4},{12,8},{16,12},{20,16},{24,20},{28,24},{32,28},{36,32}... | collective-permute-start | bytes 6291464 | tf_op jit(solution)/shard_map/ppermute | solution.py:14
  170.7 4.5 copy-start.2
  175.2 2.3 copy-start.6
  378.4 12.8 %copy-start.3 = (bf16[64,1,32,128]{0,2,1,3:T(8,128)(2,1)S(1)}, bf16[64,1,32,128]{0,2,1,3:T(8,128)(2,1)}, u32[]{:S(2)}) copy-start(bf16[64,1,32,128]{0,2,1,3:T(8,128)(2,1)} %get-tuple-element.12) | copy-start | bytes 1572868
  520.4 11.4 %slice-start = ((s8[8388608]{0:T(1024)(128)(4,1)}), s8[4194304]{0:T(1024)(128)(4,1)S(1)}, s32[]{:S(2)}) async-start(s8[8388608]{0:T(1024)(128)(4,1)} %bitcast.47), calls=%async_computation.2 | async-start | bytes 8388608
  524.4 7.3 slice-start.1
  570.1 178.9 %copy-start.1 = (bf16[64,32,512]{2,1,0:T(8,128)(2,1)S(1)}, bf16[64,32,512]{2,1,0:T(8,128)(2,1)}, u32[]{:S(2)}) copy-start(bf16[64,32,512]{2,1,0:T(8,128)(2,1)} %param.1) | copy-start | bytes 6291460
Sparse Core Ops, SparseCore 0:
  570.2 170.6 reduce-scatter.1
where the time goes:
time: 765 us; the launch traced here: 756 us
  local copies, waits for them, and re-layouts  365 us (48%)
  waiting for transfers between devices  310 us (41%)
  other arithmetic  31.5 us (4%)
  matrix products  30 us (4%)
  between operations  13.8 us (2%)
    reduce_scatter x1, waiting for transfers between devices, per_device(): lax.psum_scatter(term.astype(jnp.bfloat16), 'tm', scatter_dimension=2, ti...  171 us
    ppermute x4, waiting for transfers between devices, passed_along(): return lax.ppermute(block, axis, route)  139 us
    slice x4, local copies, waits for them, and re-layouts, segment_stack(): real_band = lag_band(products[:, :channels], lags)  99.9 us
    reshape x4, local copies, waits for them, and re-layouts, lag_band(): return flattened.reshape(leading + (channels, columns + 1))[..., :lags]  41.2 us
    unnamed x26, local copies, waits for them, and re-layouts  41.1 us
    slice x2, local copies, waits for them, and re-layouts, segment_stack(): imag_band = lag_band(products[:, channels:], lags)  38.4 us
    pad x4, local copies, waits for them, and re-layouts, lag_band(): flattened = jnp.pad(flattened, pad_spec)  35.6 us
    dot_general x2, matrix products, segment_stack(): jnp.einsum('apwf,jpwf->faj', left_rows, reach, preferred_element_type=jnp...  28.7 us
  transfers between devices with their start and end apart: 5, of which 4 were waited for; matrix products, arithmetic and copies ran while one was open for 7% of the time, Pallas kernels for 0%

commit v1 on v0

v1 whole, which is shorter than its diff:
```python
import math

import jax
import jax.numpy as jnp
import numpy as np
from jax import lax
from jax.experimental import pallas as pl
from jax.experimental.pallas import tpu as pltpu
from jax.sharding import PartitionSpec as P

MESH = pl.DeviceIdType.MESH

CH = 64
LAG = 256
BINS = 256
WIN = 32
NSAMP = 512
SEG = 4
BAND = BINS // SEG
FCH = 8
NCH = BAND // FCH
NBLK = LAG // CH + 1
ROWY = 4
SCALE = 1.0 / math.sqrt(WIN * SEG)


def kernel_rows():
    samples = np.arange(NSAMP, dtype=np.int32)
    freqs = np.arange(BINS, dtype=np.int32)
    phase = (samples[:, None] * freqs[None, :]) % NSAMP
    angles = np.float32(2.0 * math.pi / NSAMP) * phase.astype(np.float32)
    taper = np.float32(0.5) - np.float32(0.5) * np.cos(
        np.float32(2.0 * math.pi / NSAMP) * samples.astype(np.float32)
    )
    cosines = taper[:, None] * np.cos(angles)
    sines = -taper[:, None] * np.sin(angles)
    table = np.stack([cosines.T, sines.T], axis=0).astype(np.float32)
    table = table.reshape(2, SEG, NCH, FCH, NSAMP).transpose(1, 2, 0, 3, 4)
    return table.reshape(2 * BINS, NSAMP).astype(jnp.bfloat16)


def stack_kernel(tr_ref, kt_ref, out_ref, wt, rx, ball, relay, prod, obuf,
                 a2a_send, a2a_recv, own_sem, blk_send, blk_recv, out_sem):
    chain = lax.axis_index("chain")
    me = lax.axis_index("tm")
    n_chain = lax.axis_size("chain")
    y = lax.rem(chain, ROWY)

    def peer(delta):
        return lax.rem(me + delta, SEG)

    first = y == 0
    last = y == ROWY - 1
    src1 = jnp.where(last, chain - (ROWY - 1), chain + 1)
    src3 = jnp.where(first, chain + (ROWY - 1), chain - 1)
    dst1 = jnp.where(first, chain + (ROWY - 1), chain - 1)
    dst3 = jnp.where(last, chain - (ROWY - 1), chain + 1)
    has4 = chain + ROWY < n_chain
    to4 = chain >= ROWY
    has2 = chain + 1 < n_chain
    to2 = chain >= 1

    barrier = pltpu.get_barrier_semaphore()

    def greet(c, t):
        pl.semaphore_signal(barrier, inc=1, device_id=(c, t), device_id_type=MESH)

    for delta in (1, 2, 3):
        greet(chain, peer(delta))
    greet(src1, me)
    greet(src3, me)
    pl.when(has4)(lambda: greet(chain + ROWY, me))
    pl.when(has2)(lambda: greet(chain + 1, me))

    cols = 256
    chans = cols // WIN

    def whiten(j, carry):
        tr = tr_ref[pl.ds(chans * j, chans)].reshape(cols, NSAMP)
        spec = lax.dot_general(kt_ref[...], tr, (((1,), (1,)), ((), ())),
                               preferred_element_type=jnp.float32)
        spec = spec.reshape(SEG * NCH, 2, FCH, cols)
        re = spec[:, 0]
        im = spec[:, 1]
        mag = jnp.sqrt(re * re + im * im)
        level = jnp.sum(mag, axis=(0, 1), keepdims=True) * (1.0 / BINS)
        inv = 1.0 / (mag + 0.1 * (level + 1e-6))
        white = jnp.stack([re * inv, im * inv], axis=1)
        white = white.reshape(SEG, NCH, 2 * FCH, cols).astype(jnp.bfloat16)
        wt[:, :, :, pl.ds(pl.multiple_of(cols * j, cols), cols)] = white
        return carry

    lax.fori_loop(0, CH // chans, whiten, 0)

    n_wait = 5 + to4.astype(jnp.int32) + to2.astype(jnp.int32)
    pl.semaphore_wait(barrier, n_wait)

    def a2a_copy(delta, k):
        return pltpu.make_async_remote_copy(
            src_ref=wt.at[peer(delta), k], dst_ref=rx.at[me, k],
            send_sem=a2a_send.at[delta - 1, k], recv_sem=a2a_recv.at[delta - 1, k],
            device_id=(chain, peer(delta)), device_id_type=MESH)

    def own_copy():
        return pltpu.make_async_copy(wt.at[me], rx.at[me], own_sem)

    own_copy().start()

    def start_a2a(k, carry):
        for delta in (1, 2, 3):
            a2a_copy(delta, k).start()
        return carry

    lax.fori_loop(0, NCH, start_a2a, 0)

    @pl.when(jnp.logical_not(has4))
    def _():
        ball[:, 4 * CH:5 * CH, :] = jnp.zeros((BAND, CH, LAG), jnp.bfloat16)

    @pl.when(jnp.logical_not(has2))
    def _():
        ball[:, 2 * CH:3 * CH, :] = jnp.zeros((BAND, CH, LAG), jnp.bfloat16)

    own_copy().wait()

    def block(d, k):
        return ball.at[pl.ds(FCH * k, FCH), pl.ds(CH * d, CH), :]

    def block_copy(src, d, k, target):
        return pltpu.make_async_remote_copy(
            src_ref=block(src, k), dst_ref=block(d, k),
            send_sem=blk_send.at[d - 1, k], recv_sem=blk_recv.at[d - 1, k],
            device_id=(target, me), device_id_type=MESH)

    def relayout(k):
        lane = lax.broadcasted_iota(jnp.int32, (2 * FCH, 128), 1)
        low = lane < 64
        even = lax.rem(lane // 32, 2) == 0

        def group(c4, carry):
            at = pl.ds(pl.multiple_of(c4 * 128, 128), 128)
            x = [rx[h, k, :, at].astype(jnp.float32) for h in range(SEG)]
            a0 = jnp.where(low, x[0], pltpu.roll(x[2], 64, 1))
            a2 = jnp.where(low, pltpu.roll(x[0], 64, 1), x[2])
            a1 = jnp.where(low, x[1], pltpu.roll(x[3], 64, 1))
            a3 = jnp.where(low, pltpu.roll(x[1], 64, 1), x[3])
            o0 = jnp.where(even, a0, pltpu.roll(a1, 32, 1))
            o1 = jnp.where(even, pltpu.roll(a0, 96, 1), a1)
            o2 = jnp.where(even, a2, pltpu.roll(a3, 32, 1))
            o3 = jnp.where(even, pltpu.roll(a2, 96, 1), a3)
            for c, o in enumerate((o0, o1, o2, o3)):
                rows = pl.ds(pl.multiple_of((c4 * 4 + c) * FCH, FCH), FCH)
                relay[0, rows, :] = o[:FCH]
                relay[1, rows, :] = o[FCH:]
            return carry

        lax.fori_loop(0, CH // 4, group, 0)
        for f in range(FCH):
            for p in range(2):
                v = relay[p, pl.ds(f, CH, stride=FCH), :]
                ball[FCH * k + f, 0:CH, 128 * p:128 * p + 128] = v.astype(jnp.bfloat16)

    def products(k, slot):
        def one_bin(f, carry):
            fi = FCH * k + f
            x = ball[fi, 0:CH, :]
            re = x[:, :128]
            im = x[:, 128:]
            left = jnp.concatenate(
                [x, jnp.concatenate([im, -re], axis=1)], axis=0)
            pr = lax.dot_general(left, ball[fi], (((1,), (1,)), ((), ())),
                                 preferred_element_type=jnp.float32) * SCALE
            pr = jnp.concatenate([pr, jnp.zeros((2 * CH, 64), jnp.float32)], axis=1)
            for q in range(2):
                half = pr[CH * q:CH * q + CH]
                row = lax.broadcasted_iota(jnp.int32, half.shape, 0)
                for bit in range(6):
                    moved = pltpu.roll(half, half.shape[1] - (1 << bit), 1)
                    half = jnp.where(lax.rem(row // (1 << bit), 2) == 1, moved, half)
                for t in range(LAG // 128):
                    prod[q, t, pl.ds(pl.multiple_of(f * CH, CH), CH), :] = half[:, 128 * t:128 * t + 128]
            return carry

        lax.fori_loop(0, FCH, one_bin, 0)

        def one_channel(c, carry):
            for q in range(2):
                for t in range(LAG // 128):
                    obuf[slot, c, q, :, 128 * t:128 * t + 128] = prod[
                        q, t, pl.ds(c, FCH, stride=CH), :]
            return carry

        lax.fori_loop(0, CH, one_channel, 0)

    def out_copy(k, slot):
        return pltpu.make_async_copy(
            obuf.at[slot], out_ref.at[:, :, pl.ds(FCH * k, FCH), :], out_sem.at[slot])

    def step(s, carry):
        @pl.when(s < NCH)
        def _():
            k = s
            for delta in (1, 2, 3):
                a2a_copy(delta, k).wait_recv()
            relayout(k)
            pl.when(to4)(lambda: block_copy(0, 4, k, chain - ROWY).start())
            pl.when(jnp.logical_not(first))(lambda: block_copy(0, 1, k, dst1).start())
            pl.when(last)(lambda: block_copy(0, 3, k, dst3).start())

        @pl.when(jnp.logical_and(s >= 2, s < NCH + 2))
        def _():
            k = s - 2
            pl.when(has4)(lambda: block_copy(0, 4, k, chain).wait_recv())
            pl.when(jnp.logical_not(last))(lambda: block_copy(4, 3, k, dst3).start())
            pl.when(first)(lambda: block_copy(4, 1, k, dst1).start())

        @pl.when(jnp.logical_and(s >= 3, s < NCH + 3))
        def _():
            k = s - 3
            block_copy(0, 1, k, dst1).wait_recv()
            pl.when(to2)(lambda: block_copy(1, 2, k, chain - 1).start())

        @pl.when(s >= 5)
        def _():
            k = s - 5
            slot = lax.rem(k, 2)
            block_copy(0, 3, k, dst3).wait_recv()
            pl.when(has2)(lambda: block_copy(1, 2, k, chain).wait_recv())
            pl.when(k >= 2)(lambda: out_copy(k - 2, slot).wait())
            products(k, slot)
            out_copy(k, slot).start()
        return carry

    lax.fori_loop(0, NCH + 5, step, 0)

    out_copy(NCH - 2, (NCH - 2) % 2).wait()
    out_copy(NCH - 1, (NCH - 1) % 2).wait()

    def drain(k, carry):
        for delta in (1, 2, 3):
            a2a_copy(delta, k).wait_send()
        pl.when(to4)(lambda: block_copy(0, 4, k, chain - ROWY).wait_send())
        block_copy(0, 1, k, dst1).wait_send()
        block_copy(0, 3, k, dst3).wait_send()
        pl.when(to2)(lambda: block_copy(1, 2, k, chain - 1).wait_send())
        return carry

    lax.fori_loop(0, NCH, drain, 0)


def per_device(traces):
    table = jnp.asarray(kernel_rows())
    dma = pltpu.SemaphoreType.DMA
    return pl.pallas_call(
        stack_kernel,
        out_shape=jax.ShapeDtypeStruct((CH, 2, BAND, LAG), jnp.float32),
        in_specs=[pl.BlockSpec(memory_space=pltpu.VMEM)] * 2,
        out_specs=pl.BlockSpec(memory_space=pl.ANY),
        scratch_shapes=[
            pltpu.VMEM((SEG, NCH, 2 * FCH, CH * WIN), jnp.bfloat16),
            pltpu.VMEM((SEG, NCH, 2 * FCH, CH * WIN), jnp.bfloat16),
            pltpu.VMEM((BAND, NBLK * CH, 2 * WIN * SEG), jnp.bfloat16),
            pltpu.VMEM((2, CH * FCH, 128), jnp.float32),
            pltpu.VMEM((2, LAG // 128, FCH * CH, 128), jnp.float32),
            pltpu.VMEM((2, CH, 2, FCH, LAG), jnp.float32),
            dma((3, NCH)), dma((3, NCH)), dma, dma((4, NCH)), dma((4, NCH)), dma((2,)),
        ],
        compiler_params=pltpu.CompilerParams(
            collective_id=0, has_side_effects=True, vmem_limit_bytes=48 << 20),
    )(traces, table)


def solution(mesh):
    return jax.shard_map(
        per_device,
        mesh=mesh,
        in_specs=(P("chain", "tm", None),),
        out_specs=P("chain", None, "tm", None),
        check_vma=False,
    )
```

time: 765 us -> 152 us (0.20)
  the two profiles are of different devices: /device:TPU:1 before, /device:TPU:122 now
where the time goes in v1:
time: 152 us; the launch traced here: 151 us
  Pallas kernels  141 us (93%)
  local copies, waits for them, and re-layouts  10.5 us (7%)
    pallas_call x1, Pallas kernels, per_device(): pl.pallas_call(stack_kernel, out_shape=jax.ShapeDtypeStruct((CH, 2, BAND,...  141 us
    unnamed x5, local copies, waits for them, and re-layouts  10.5 us

profile of v1, /device:TPU:122, one launch (start us, length us, event | category | flops | bytes accessed | tf_op | source)
XLA Modules:
  0.0 151.4 jit_solution(10447406693944788494)
XLA Ops:
  0.0 0.0 copy-start
  0.0 1.6 %copy-done = bf16[64,32,512]{2,1,0:T(8,128)(2,1)S(1)} copy-done((bf16[64,32,512]{2,1,0:T(8,128)(2,1)S(1)}, bf16[64,32,512]{2,1,0:T(8,128)(2,1)}, u32[]{:S(2)}) %copy-start) | copy-done | bytes 2097176
  1.6 0.0 copy-start.1
  1.6 1.0 copy-done.1
  2.6 140.8 %shard_map.28 = f32[64,2,64,256]{3,2,1,0:T(8,128)} custom-call(bf16[64,32,512]{2,1,0:T(8,128)(2,1)S(1)} %copy-done, bf16[512,512]{1,0:T(8,128)(2,1)S(1)} %copy-done.1), custom_call_target="tpu_custom_call" | custom-call | tf_op jit(solution)/shard_map/pallas_call | solution.py:254
  143.5 7.9 %copy.4 = f32[64,2,64,256]{3,2,1,0:T(8,128)} copy(f32[64,2,64,256]{3,2,1,0:T(8,128)} %shard_map.28) | data formatting | bytes 16777216
Async XLA Ops:
  0.0 1.6 %copy-start = (bf16[64,32,512]{2,1,0:T(8,128)(2,1)S(1)}, bf16[64,32,512]{2,1,0:T(8,128)(2,1)}, u32[]{:S(2)}) copy-start(bf16[64,32,512]{2,1,0:T(8,128)(2,1)} %tr_ref.1) | copy-start | bytes 6291460
  1.6 1.0 copy-start.1

commit v2 on v1

v2 whole, which is shorter than its diff:
```python
import math

import jax
import jax.numpy as jnp
import numpy as np
from jax import lax
from jax.experimental import pallas as pl
from jax.experimental.pallas import tpu as pltpu
from jax.sharding import PartitionSpec as P

MESH = pl.DeviceIdType.MESH
BF16 = jnp.bfloat16
F32 = jnp.float32

CH = 64
LAG = 256
BINS = 256
WIN = 32
NSAMP = 512
SEG = 4
BAND = BINS // SEG
FCH = 8
NCH = BAND // FCH
DEPTH = 2 * WIN * SEG
ROWY = 4
SCALE = 1.0 / math.sqrt(WIN * SEG)
FETCHED = ((), (2, 4, 6), (2, 4, 6), (2, 5))
FETCHED_FAR = ((), (2, 4, 6), (2, 4, 6), (2,5))
FETCHED_NEAR = (0,1,3,5,7)
AHEAD = 3
OWN_AT = (0, 2, 1)
TWO_AT = (4, 2, 1)
TWO_LAST_AT = (4, 2, 1)
PASS_AT = (2, 2, 1)
FOUR_AT = (2, 2, 1)
PAIRS_AT = (6, 2, 1)
FINISH_AT = (10, 2, 1)
FAR_LATE = 0


def tick_of(plan, k):
    offset, num, den = plan
    return offset + k * num // den


def chunk_at(plan, t, late=0):
    offset, num, den = plan
    offset = offset + late
    k = ((t - offset) * den + num - 1) // num
    fits = jnp.logical_and(t >= offset, k < NCH)
    return k, jnp.logical_and(fits, offset + k * num // den == t)


OWN, UP1, UP4, UP3, UP2 = 0, CH, 2 * CH, 3 * CH, 4 * CH


def kernel_rows():
    samples = np.arange(NSAMP, dtype=np.int32)
    freqs = np.arange(BINS, dtype=np.int32)
    phase = (samples[:, None] * freqs[None, :]) % NSAMP
    angles = np.float32(2.0 * math.pi / NSAMP) * phase.astype(np.float32)
    taper = np.float32(0.5) - np.float32(0.5) * np.cos(
        np.float32(2.0 * math.pi / NSAMP) * samples.astype(np.float32)
    )
    cosines = taper[:, None] * np.cos(angles)
    sines = -taper[:, None] * np.sin(angles)
    table = np.stack([cosines.T, sines.T], axis=0).astype(np.float32)
    table = table.reshape(2, SEG, NCH, FCH, NSAMP).transpose(1, 2, 0, 3, 4)
    return table.reshape(2 * BINS, NSAMP).astype(jnp.bfloat16)


def dot_nt(a, b):
    return lax.dot_general(a, b, (((1,), (1,)), ((), ())), preferred_element_type=F32)


def stack_kernel(tr_hbm, kt_hbm, out_ref, tr_ref, kt_ref, wt, rx, ball, lrev, osend, orecv,
                 stage, relay, prod, obuf, in_sem, a2a_send, a2a_recv, own_sem, blk_send, blk_recv,
                 hi_send, hi_recv, pass_send, stage_recv,
                 o_send, o_recv, out_sem):
    chain = lax.axis_index("chain")
    me = lax.axis_index("tm")
    n_chain = lax.axis_size("chain")
    y = lax.rem(chain, ROWY)

    cols = 256
    chans = cols // WIN
    n_in = CH // chans

    def in_copy(j):
        rows = pl.ds(chans * j, chans)
        return pltpu.make_async_copy(tr_hbm.at[rows], tr_ref.at[rows], in_sem.at[j])

    def table_copy():
        return pltpu.make_async_copy(kt_hbm, kt_ref, in_sem.at[n_in])

    table_copy().start()
    for j in range(n_in):
        in_copy(j).start()

    def peer(delta):
        return lax.rem(me + delta, SEG)

    def along(delta):
        return lax.rem(chain + n_chain + delta, n_chain)

    def bits(chunks):
        return sum(1 << k for k in chunks)

    def fetched_set(i):
        place = lax.rem(i, ROWY)
        depth = lax.rem(i // ROWY, ROWY)
        mask = jnp.int32(0)
        for p in range(ROWY):
            there = place == p
            mask = jnp.where(there, bits(FETCHED[p]), mask)
            mask = jnp.where(jnp.logical_and(there, depth == ROWY - 1),
                             bits(FETCHED_FAR[p]), mask)
        return jnp.where(jnp.logical_and(place == 0, depth == 0), bits(FETCHED_NEAR), mask)

    here, below, above = chain, along(-1), along(1)
    fetched_sets = [(i, fetched_set(i)) for i in (here, below, above, 0)]

    def is_fetched(i, k):
        mask = [m for j, m in fetched_sets if j is i][0]
        return lax.rem(lax.shift_right_logical(mask, jnp.int32(k)), 2) == 1

    def paired(i, k):
        return jnp.logical_not(is_fetched(i, k))

    def gets1(i, k):
        return jnp.logical_or(i + 1 < n_chain, paired(0, k))

    def gets2(i, k):
        return jnp.logical_and(i + 2 < n_chain, is_fetched(i, k))

    def gets3(i, k):
        return jnp.logical_or(i + 3 < n_chain, jnp.logical_and(i == n_chain - 1, paired(0, k)))

    def gets4(i, k):
        extra = jnp.logical_or(i == n_chain - 4, i == n_chain - 2)
        return jnp.logical_or(i + 4 < n_chain, jnp.logical_and(extra, paired(0, k)))

    def gets_pairs(i, k):
        return jnp.logical_and(i + 2 < n_chain, paired(i, k))

    first = y == 0
    last = y == ROWY - 1
    src1 = jnp.where(last, chain - (ROWY - 1), chain + 1)
    src3 = jnp.where(first, chain + (ROWY - 1), chain - 1)
    dst1 = jnp.where(first, chain + (ROWY - 1), chain - 1)
    dst3 = jnp.where(last, chain - (ROWY - 1), chain + 1)

    barrier = pltpu.get_barrier_semaphore()

    def greet(c, t):
        pl.semaphore_signal(barrier, inc=1, device_id=(c, t), device_id_type=MESH)

    for delta in (1, 2, 3):
        greet(chain, peer(delta))
    for source in (src1, src3, along(ROWY), along(1), along(-1)):
        greet(source, me)
    greet(along(-3 * ROWY), me)
    greet(along(n_chain // 2), me)

    table_copy().wait()

    def whiten(j, carry):
        in_copy(j).wait()
        tr = tr_ref[pl.ds(chans * j, chans)].reshape(cols, NSAMP)
        spec = dot_nt(kt_ref[...], tr).reshape(SEG * NCH, 2, FCH, cols)
        re = spec[:, 0]
        im = spec[:, 1]
        mag = jnp.sqrt(re * re + im * im)
        level = jnp.sum(mag, axis=(0, 1), keepdims=True) * (1.0 / BINS)
        inv = 1.0 / (mag + 0.1 * (level + 1e-6))
        white = jnp.stack([re * inv, im * inv], axis=1)
        white = white.reshape(SEG, NCH, 2 * FCH, cols).astype(BF16)
        wt[:, :, :, pl.ds(pl.multiple_of(cols * j, cols), cols)] = white
        return carry

    lax.fori_loop(0, n_in, whiten, 0)

    pl.semaphore_wait(barrier, 10)

    def a2a_copy(delta, k):
        return pltpu.make_async_remote_copy(
            src_ref=wt.at[peer(delta), k], dst_ref=rx.at[me, k],
            send_sem=a2a_send.at[delta - 1, k], recv_sem=a2a_recv.at[delta - 1, k],
            device_id=(chain, peer(delta)), device_id_type=MESH)

    def own_copy():
        return pltpu.make_async_copy(wt.at[me], rx.at[me], own_sem)

    own_copy().start()

    def start_a2a(k, carry):
        for delta in (1, 2, 3):
            a2a_copy(delta, k).start()
        return carry

    lax.fori_loop(0, AHEAD, start_a2a, 0)
    own_copy().wait()

    def block(rows, k):
        return ball.at[pl.ds(FCH * k, FCH), pl.ds(rows, CH), :]

    def block_copy(src, dst, k, target):
        return pltpu.make_async_remote_copy(
            src_ref=block(src, k), dst_ref=block(dst, k),
            send_sem=blk_send.at[dst // CH - 1, k], recv_sem=blk_recv.at[dst // CH - 1, k],
            device_id=(target, me), device_id_type=MESH)

    HALF = FCH // 2
    depth = lax.rem(chain // ROWY, ROWY)
    upper = chain >= n_chain // 2
    far_from = jnp.logical_and(upper, depth == 0)
    passes = jnp.logical_and(upper, depth == ROWY - 1)
    far_to = depth == ROWY - 1

    def half_copy(src, dst, send, recv, target):
        return pltpu.make_async_remote_copy(
            src_ref=src, dst_ref=dst, send_sem=send, recv_sem=recv,
            device_id=target, device_id_type=MESH)

    def bins_of(rows, k, half):
        return ball.at[pl.ds(FCH * k + HALF * half, HALF), pl.ds(rows, CH), :]

    def low4(k, target):
        return half_copy(bins_of(OWN, k, 0), bins_of(UP4, k, 0),
                         blk_send.at[1, k], blk_recv.at[1, k], (target, me))

    def high4(k, target):
        return half_copy(bins_of(OWN, k, 1), bins_of(UP4, k, 1),
                         hi_send.at[k], hi_recv.at[k], (target, me))

    def stage4(k):
        return half_copy(bins_of(OWN, k, 1), stage.at[k],
                         hi_send.at[k], stage_recv.at[k], (along(3 * ROWY), me))

    def pass4(k):
        return half_copy(stage.at[k], bins_of(UP4, k, 1),
                         pass_send.at[k], hi_recv.at[k], (along(n_chain // 2), me))

    def product_copy(k):
        bins = pl.ds(FCH * k, FCH)
        return pltpu.make_async_remote_copy(
            src_ref=osend.at[bins], dst_ref=orecv.at[bins],
            send_sem=o_send.at[k], recv_sem=o_recv.at[k],
            device_id=(along(1), me), device_id_type=MESH)

    rows64 = lax.broadcasted_iota(jnp.int32, (CH, CH), 0)
    cols64 = lax.broadcasted_iota(jnp.int32, (CH, CH), 1)
    flip = (rows64 + cols64 == CH - 1).astype(F32).astype(BF16)

    def flipped(x):
        return jnp.dot(flip, x, preferred_element_type=F32).astype(BF16)

    def relayout(k):
        lane = lax.broadcasted_iota(jnp.int32, (2 * FCH, 128), 1)
        low = lane < 64
        even = lax.rem(lane // 32, 2) == 0

        def group(c4):
            at = pl.ds(pl.multiple_of(c4 * 128, 128), 128)
            x = [rx[h, k, :, at].astype(F32) for h in range(SEG)]
            a0 = jnp.where(low, x[0], pltpu.roll(x[2], 64, 1))
            a2 = jnp.where(low, pltpu.roll(x[0], 64, 1), x[2])
            a1 = jnp.where(low, x[1], pltpu.roll(x[3], 64, 1))
            a3 = jnp.where(low, pltpu.roll(x[1], 64, 1), x[3])
            o0 = jnp.where(even, a0, pltpu.roll(a1, 32, 1))
            o1 = jnp.where(even, pltpu.roll(a0, 96, 1), a1)
            o2 = jnp.where(even, a2, pltpu.roll(a3, 32, 1))
            o3 = jnp.where(even, pltpu.roll(a2, 96, 1), a3)
            for c, o in enumerate((o0, o1, o2, o3)):
                rows = pl.ds(pl.multiple_of((c4 * 4 + c) * FCH, FCH), FCH)
                relay[0, rows, :] = o[:FCH]
                relay[1, rows, :] = o[FCH:]

        def groups(i, carry):
            for u in range(4):
                group(i * 4 + u)
            return carry

        lax.fori_loop(0, CH // 16, groups, 0)
        for f in range(FCH):
            halves = [relay[p, pl.ds(f, CH, stride=FCH), :] for p in range(2)]
            x = jnp.concatenate(halves, axis=1).astype(BF16)
            ball[FCH * k + f, OWN:OWN + CH, :] = x
            lrev[FCH * k + f] = flipped(x)

    def neighbour_products(k):
        def bins(i, carry):
            for u in range(4):
                fi = FCH * k + i * 4 + u
                left = flipped(ball[fi, UP1:UP1 + CH, :])
                right = ball[fi, UP3:UP3 + CH, :]
                turned = jnp.concatenate([-right[:, 128:], right[:, :128]], axis=1)
                both = jnp.concatenate([right, turned], axis=0)
                osend[fi] = dot_nt(left, both).astype(BF16)
            return carry

        lax.fori_loop(0, FCH // 4, bins, 0)

    lane = lax.broadcasted_iota(jnp.int32, (CH, 128), 1)
    low = lane < 64
    lane3 = lax.broadcasted_iota(jnp.int32, (1, 384), 1)
    inside = (chain + lane3 // CH) < n_chain

    def products(k, slot, fetched):
        def one_bin(f):
            fi = FCH * k + f
            x = lrev[fi]
            turned = jnp.concatenate([x[:, 128:], -x[:, :128]], axis=1)
            left = jnp.concatenate([x, turned], axis=0)
            if fetched:
                pr = dot_nt(left, ball[fi])
                pad = jnp.zeros((2 * CH, 64), F32)
                two = jnp.concatenate([pr[:, 256:], pad], axis=1)
                two = [two[:CH], two[CH:]]
            else:
                pr = dot_nt(left, ball[fi, :256, :])
                o = orecv[fi].astype(F32)
                two = [o, pltpu.roll(o, 64, 1)]
            for q in range(2):
                p0 = pr[CH * q:CH * q + CH, :128]
                p1 = pr[CH * q:CH * q + CH, 128:256]
                mid = jnp.where(low, two[q], p1)
                full = jnp.concatenate([p0, mid, p1], axis=1) * SCALE
                full = jnp.where(inside, full, 0.0)
                full = pltpu.roll(full, 384 - (CH - 1), 1, stride=1, stride_axis=0)
                for t in range(LAG // 128):
                    prod[q, t, pl.ds(f * CH, CH), :] = full[:, 128 * t:128 * t + 128]

        for f in range(FCH):
            one_bin(f)

    def to_rows(slot):
        def channels(i, carry):
            for u in range(16):
                c = i * 16 + u
                for q in range(2):
                    for t in range(LAG // 128):
                        obuf[slot, c, FCH * q:FCH * q + FCH, 128 * t:128 * t + 128] = prod[
                            q, t, pl.ds(CH - 1 - c, FCH, stride=CH), :].astype(BF16)
            return carry

        lax.fori_loop(0, CH // 16, channels, 0)

    def out_copy(k, slot):
        return pltpu.make_async_copy(
            obuf.at[slot], out_ref.at[k], out_sem.at[slot])

    def both(a, b):
        return jnp.logical_and(a, b)

    send1_own = jnp.logical_not(first)
    send3_own = last

    late = jnp.where(far_to, FAR_LATE, 0)

    def send_two(k):
        pl.when(gets1(chain, k))(lambda: block_copy(OWN, UP1, k, dst1).wait_recv())
        pl.when(gets2(below, k))(
            lambda: block_copy(UP1, UP2, k, along(-1)).start())

    def step(t, carry):
        k_own, now = chunk_at(OWN_AT, t)

        @pl.when(now)
        def _():
            k = k_own
            for delta in (1, 2, 3):
                a2a_copy(delta, k).wait_recv()
            pl.when(k + AHEAD < NCH)(lambda: start_a2a(k + AHEAD, None))
            relayout(k)

            @pl.when(gets4(along(-ROWY), k))
            def _():
                low4(k, along(-ROWY)).start()
                pl.when(far_from)(lambda: stage4(k).start())
                pl.when(jnp.logical_not(far_from))(lambda: high4(k, along(-ROWY)).start())

            pl.when(both(send1_own, gets1(dst1, k)))(
                lambda: block_copy(OWN, UP1, k, dst1).start())
            pl.when(both(send3_own, gets3(dst3, k)))(
                lambda: block_copy(OWN, UP3, k, dst3).start())

        k_two, now = chunk_at(TWO_AT, t)

        @pl.when(both(jnp.logical_not(last), now))
        def _():
            send_two(k_two)

        k_pass, now = chunk_at(PASS_AT, t, late)

        @pl.when(both(passes, now))
        def _():
            k = k_pass

            stage4(k).wait_recv()
            pass4(k).start()

        k_four, now = chunk_at(FOUR_AT, t, late)

        @pl.when(now)
        def _():
            k = k_four

            @pl.when(gets4(chain, k))
            def _():
                low4(k, chain).wait_recv()
                high4(k, chain).wait_recv()

            pl.when(both(jnp.logical_not(send3_own), gets3(dst3, k)))(
                lambda: block_copy(UP4, UP3, k, dst3).start())
            pl.when(both(jnp.logical_not(send1_own), gets1(dst1, k)))(
                lambda: block_copy(UP4, UP1, k, dst1).start())

        k_last, now = chunk_at(TWO_LAST_AT, t, late)

        @pl.when(both(last, now))
        def _():
            send_two(k_last)

        k_pairs, now = chunk_at(PAIRS_AT, t, late)

        @pl.when(now)
        def _():
            k = k_pairs
            pl.when(gets3(chain, k))(lambda: block_copy(OWN, UP3, k, dst3).wait_recv())

            @pl.when(gets_pairs(above, k))
            def _():
                neighbour_products(k)
                product_copy(k).start()

        k_finish, now = chunk_at(FINISH_AT, t, late)

        @pl.when(now)
        def _():
            k = k_finish
            slot = lax.rem(k, 2)
            pl.when(k >= 2)(lambda: out_copy(k - 2, slot).wait())
            pl.when(gets2(chain, k))(lambda: block_copy(UP1, UP2, k, chain).wait_recv())
            pl.when(gets_pairs(chain, k))(lambda: product_copy(k).wait_recv())
            pl.when(is_fetched(chain, k))(lambda: products(k, slot, True))
            pl.when(paired(chain, k))(lambda: products(k, slot, False))
            to_rows(slot)
            out_copy(k, slot).start()
        return carry

    lax.fori_loop(0, tick_of(FINISH_AT, NCH - 1) + 1 + FAR_LATE, step, 0)

    out_copy(NCH - 2, (NCH - 2) % 2).wait()
    out_copy(NCH - 1, (NCH - 1) % 2).wait()

    def drain(k, carry):
        for delta in (1, 2, 3):
            a2a_copy(delta, k).wait_send()

        @pl.when(gets4(along(-ROWY), k))
        def _():
            low4(k, along(-ROWY)).wait_send()
            high4(k, along(-ROWY)).wait_send()

        pl.when(passes)(lambda: pass4(k).wait_send())
        pl.when(gets1(dst1, k))(lambda: block_copy(OWN, UP1, k, dst1).wait_send())
        pl.when(gets3(dst3, k))(lambda: block_copy(OWN, UP3, k, dst3).wait_send())
        pl.when(gets2(below, k))(
            lambda: block_copy(UP1, UP2, k, along(-1)).wait_send())
        pl.when(gets_pairs(above, k))(lambda: product_copy(k).wait_send())
        return carry

    lax.fori_loop(0, NCH, drain, 0)


def widen_kernel(in_ref, out_ref):
    for k in range(NCH):
        for q in range(2):
            out_ref[:, q, FCH * k:FCH * k + FCH, :] = in_ref[
                k, :, FCH * q:FCH * q + FCH, :].astype(F32)


def per_device(traces):
    table = jnp.asarray(kernel_rows())
    dma = pltpu.SemaphoreType.DMA
    hbm = pl.BlockSpec(memory_space=pltpu.MemorySpace.HBM)
    stacks = pl.pallas_call(
        stack_kernel,
        out_shape=jax.ShapeDtypeStruct((NCH, CH, 2 * FCH, LAG), BF16),
        in_specs=[hbm, hbm],
        out_specs=hbm,
        scratch_shapes=[
            pltpu.VMEM((CH, WIN, NSAMP), BF16),
            pltpu.VMEM((2 * BINS, NSAMP), BF16),
            pltpu.VMEM((SEG, NCH, 2 * FCH, CH * WIN), BF16),
            pltpu.VMEM((SEG, NCH, 2 * FCH, CH * WIN), BF16),
            pltpu.VMEM((BAND, 5 * CH, DEPTH), BF16),
            pltpu.VMEM((BAND, CH, DEPTH), BF16),
            pltpu.VMEM((BAND, CH, 2 * CH), BF16),
            pltpu.VMEM((BAND, CH, 2 * CH), BF16),
            pltpu.VMEM((NCH, FCH // 2, CH, DEPTH), BF16),
            pltpu.VMEM((2, CH * FCH, 128), F32),
            pltpu.VMEM((2, LAG // 128, FCH * CH, 128), F32),
            pltpu.VMEM((2, CH, 2 * FCH, LAG), BF16),
            dma((9,)), dma((3, NCH)), dma((3, NCH)), dma, dma((4, NCH)), dma((4, NCH)),
            dma((NCH,)), dma((NCH,)), dma((NCH,)), dma((NCH,)),
            dma((NCH,)), dma((NCH,)), dma((2,)),
        ],
        compiler_params=pltpu.CompilerParams(
            collective_id=0, has_side_effects=True, vmem_limit_bytes=48 << 20),
    )(traces, table)
    part = 16
    return pl.pallas_call(
        widen_kernel,
        grid=(CH // part,),
        out_shape=jax.ShapeDtypeStruct((CH, 2, BAND, LAG), F32),
        in_specs=[pl.BlockSpec((NCH, part, 2 * FCH, LAG), lambda i: (0, i, 0, 0))],
        out_specs=pl.BlockSpec((part, 2, BAND, LAG), lambda i: (i, 0, 0, 0)),
    )(stacks)


def solution(mesh):
    return jax.shard_map(
        per_device,
        mesh=mesh,
        in_specs=(P("chain", "tm", None),),
        out_specs=P("chain", None, "tm", None),
        check_vma=False,
    )
```

time: 152 us -> 106 us (0.70)
  the two profiles are of different devices: /device:TPU:122 before, /device:TPU:6 now
where the time goes in v2:
time: 106 us
  Pallas kernels  103 us (97%)
  local copies, waits for them, and re-layouts  2.63 us (2%)
    pallas_call x1, Pallas kernels, per_device(): pl.pallas_call(stack_kernel, out_shape=jax.ShapeDtypeStruct((NCH, CH, 2 *...  97.5 us
    pallas_call x1, Pallas kernels, per_device(): pl.pallas_call(widen_kernel, grid=(CH // part,), out_shape=jax.ShapeDtype...  5.96 us
    unnamed x4, local copies, waits for them, and re-layouts  2.63 us

profile of v2, /device:TPU:6, one launch (start us, length us, event | category | flops | bytes accessed | tf_op | source)
XLA Modules:
  0.0 106.1 jit_solution(974190066933770377)
XLA Ops:
  0.0 0.0 copy-start
  0.0 1.6 %copy-done = bf16[64,32,512]{2,1,0:T(8,128)(2,1)S(1)} copy-done((bf16[64,32,512]{2,1,0:T(8,128)(2,1)S(1)}, bf16[64,32,512]{2,1,0:T(8,128)(2,1)}, u32[]{:S(2)}) %copy-start) | copy-done | bytes 2097176
  1.6 0.0 copy-start.1
  1.6 1.0 copy-done.1
  2.6 97.5 %shard_map.28.in_ref = bf16[8,64,16,256]{3,2,1,0:T(8,128)(2,1)} custom-call(bf16[64,32,512]{2,1,0:T(8,128)(2,1)S(1)} %copy-done, bf16[512,512]{1,0:T(8,128)(2,1)S(1)} %copy-done.1), custom_call_target="tpu_custom_call" | custom-call | tf_op jit(solution)/shard_map/pallas_call | solution.py:488
  100.1 6.0 %shard_map.29 = f32[64,2,64,256]{3,2,1,0:T(8,128)} custom-call(bf16[8,64,16,256]{3,2,1,0:T(8,128)(2,1)} %shard_map.28.in_ref), custom_call_target="tpu_custom_call" | custom-call | tf_op jit(solution)/shard_map/pallas_call | solution.py:514
Async XLA Ops:
  0.0 1.6 %copy-start = (bf16[64,32,512]{2,1,0:T(8,128)(2,1)S(1)}, bf16[64,32,512]{2,1,0:T(8,128)(2,1)}, u32[]{:S(2)}) copy-start(bf16[64,32,512]{2,1,0:T(8,128)(2,1)} %tr_hbm.1) | copy-start | bytes 6291460
  1.6 1.0 copy-start.1

commit v3 on v2

--- a/solution.py
+++ b/solution.py
@@ -24,7 +24,7 @@
 DEPTH = 2 * WIN * SEG
 ROWY = 4
 SCALE = 1.0 / math.sqrt(WIN * SEG)
-FETCHED = ((), (2, 4, 6), (2, 4, 6), (2, 5))
+FETCHED = ((), (2, 5), (2, 5), (3,))
 FETCHED_FAR = ((), (2, 4, 6), (2, 4, 6), (2,5))
 FETCHED_NEAR = (0,1,3,5,7)
 AHEAD = 3

time: 106 us -> 102 us (0.962)
  the two profiles are of different devices: /device:TPU:6 before, /device:TPU:1 now
where the time goes in v3:
time: 102 us; the launch traced here: 101 us
  Pallas kernels  98.6 us (97%)
  local copies, waits for them, and re-layouts  2.63 us (3%)
    pallas_call x1, Pallas kernels, per_device(): pl.pallas_call(stack_kernel, out_shape=jax.ShapeDtypeStruct((NCH, CH, 2 *...  92.7 us
    pallas_call x1, Pallas kernels, per_device(): pl.pallas_call(widen_kernel, grid=(CH // part,), out_shape=jax.ShapeDtype...  5.96 us
    unnamed x4, local copies, waits for them, and re-layouts  2.63 us

profile of v3, /device:TPU:1, one launch (start us, length us, event | category | flops | bytes accessed | tf_op | source)
XLA Modules:
  0.0 101.3 jit_solution(10279132779914387514)
XLA Ops:
  0.0 0.0 copy-start
  0.0 1.6 %copy-done = bf16[64,32,512]{2,1,0:T(8,128)(2,1)S(1)} copy-done((bf16[64,32,512]{2,1,0:T(8,128)(2,1)S(1)}, bf16[64,32,512]{2,1,0:T(8,128)(2,1)}, u32[]{:S(2)}) %copy-start) | copy-done | bytes 2097176
  1.6 0.0 copy-start.1
  1.6 1.0 %copy-done.1 = bf16[512,512]{1,0:T(8,128)(2,1)S(1)} copy-done((bf16[512,512]{1,0:T(8,128)(2,1)S(1)}, bf16[512,512]{1,0:T(8,128)(2,1)}, u32[]{:S(2)}) %copy-start.1) | copy-done | bytes 524312
  2.6 92.7 %shard_map.28.in_ref = bf16[8,64,16,256]{3,2,1,0:T(8,128)(2,1)} custom-call(bf16[64,32,512]{2,1,0:T(8,128)(2,1)S(1)} %copy-done, bf16[512,512]{1,0:T(8,128)(2,1)S(1)} %copy-done.1), custom_call_target="tpu_custom_call" | custom-call | tf_op jit(solution)/shard_map/pallas_call | solution.py:488
  95.3 6.0 %shard_map.29 = f32[64,2,64,256]{3,2,1,0:T(8,128)} custom-call(bf16[8,64,16,256]{3,2,1,0:T(8,128)(2,1)} %shard_map.28.in_ref), custom_call_target="tpu_custom_call" | custom-call | tf_op jit(solution)/shard_map/pallas_call | solution.py:514
Async XLA Ops:
  0.0 1.6 %copy-start = (bf16[64,32,512]{2,1,0:T(8,128)(2,1)S(1)}, bf16[64,32,512]{2,1,0:T(8,128)(2,1)}, u32[]{:S(2)}) copy-start(bf16[64,32,512]{2,1,0:T(8,128)(2,1)} %tr_hbm.1) | copy-start | bytes 6291460
  1.6 1.0 %copy-start.1 = (bf16[512,512]{1,0:T(8,128)(2,1)S(1)}, bf16[512,512]{1,0:T(8,128)(2,1)}, u32[]{:S(2)}) copy-start(bf16[512,512]{1,0:T(8,128)(2,1)} %constant.2.clone.kt_hbm) | copy-start | bytes 1572868

commit v4 on v3

--- a/solution.py
+++ b/solution.py
@@ -27,7 +27,7 @@
 FETCHED = ((), (2, 5), (2, 5), (3,))
 FETCHED_FAR = ((), (2, 4, 6), (2, 4, 6), (2,5))
 FETCHED_NEAR = (0,1,3,5,7)
-AHEAD = 3
+AHEAD = 2
 OWN_AT = (0, 2, 1)
 TWO_AT = (4, 2, 1)
 TWO_LAST_AT = (4, 2, 1)
@@ -74,9 +74,9 @@
 
 
 def stack_kernel(tr_hbm, kt_hbm, out_ref, tr_ref, kt_ref, wt, rx, ball, lrev, osend, orecv,
-                 stage, relay, prod, obuf, in_sem, a2a_send, a2a_recv, own_sem, blk_send, blk_recv,
+                 stage, relay, prod, in_sem, a2a_send, a2a_recv, own_sem, blk_send, blk_recv,
                  hi_send, hi_recv, pass_send, stage_recv,
-                 o_send, o_recv, out_sem):
+                 o_send, o_recv):
     chain = lax.axis_index("chain")
     me = lax.axis_index("tm")
     n_chain = lax.axis_size("chain")
@@ -306,7 +306,7 @@
     lane3 = lax.broadcasted_iota(jnp.int32, (1, 384), 1)
     inside = (chain + lane3 // CH) < n_chain
 
-    def products(k, slot, fetched):
+    def products(k, fetched):
         def one_bin(f):
             fi = FCH * k + f
             x = lrev[fi]
@@ -334,21 +334,17 @@
         for f in range(FCH):
             one_bin(f)
 
-    def to_rows(slot):
+    def to_rows(k):
         def channels(i, carry):
             for u in range(16):
                 c = i * 16 + u
                 for q in range(2):
                     for t in range(LAG // 128):
-                        obuf[slot, c, FCH * q:FCH * q + FCH, 128 * t:128 * t + 128] = prod[
+                        out_ref[k, c, FCH * q:FCH * q + FCH, 128 * t:128 * t + 128] = prod[
                             q, t, pl.ds(CH - 1 - c, FCH, stride=CH), :].astype(BF16)
             return carry
 
         lax.fori_loop(0, CH // 16, channels, 0)
-
-    def out_copy(k, slot):
-        return pltpu.make_async_copy(
-            obuf.at[slot], out_ref.at[k], out_sem.at[slot])
 
     def both(a, b):
         return jnp.logical_and(a, b)
@@ -439,20 +435,15 @@
         @pl.when(now)
         def _():
             k = k_finish
-            slot = lax.rem(k, 2)
-            pl.when(k >= 2)(lambda: out_copy(k - 2, slot).wait())
             pl.when(gets2(chain, k))(lambda: block_copy(UP1, UP2, k, chain).wait_recv())
             pl.when(gets_pairs(chain, k))(lambda: product_copy(k).wait_recv())
-            pl.when(is_fetched(chain, k))(lambda: products(k, slot, True))
-            pl.when(paired(chain, k))(lambda: products(k, slot, False))
-            to_rows(slot)
-            out_copy(k, slot).start()
+            pl.when(is_fetched(chain, k))(lambda: products(k, True))
+            pl.when(paired(chain, k))(lambda: products(k, False))
+            to_rows(k)
         return carry
 
     lax.fori_loop(0, tick_of(FINISH_AT, NCH - 1) + 1 + FAR_LATE, step, 0)
 
-    out_copy(NCH - 2, (NCH - 2) % 2).wait()
-    out_copy(NCH - 1, (NCH - 1) % 2).wait()
 
     def drain(k, carry):
         for delta in (1, 2, 3):
@@ -489,7 +480,7 @@
         stack_kernel,
         out_shape=jax.ShapeDtypeStruct((NCH, CH, 2 * FCH, LAG), BF16),
         in_specs=[hbm, hbm],
-        out_specs=hbm,
+        out_specs=pl.BlockSpec(memory_space=pltpu.VMEM),
         scratch_shapes=[
             pltpu.VMEM((CH, WIN, NSAMP), BF16),
             pltpu.VMEM((2 * BINS, NSAMP), BF16),
@@ -502,13 +493,12 @@
             pltpu.VMEM((NCH, FCH // 2, CH, DEPTH), BF16),
             pltpu.VMEM((2, CH * FCH, 128), F32),
             pltpu.VMEM((2, LAG // 128, FCH * CH, 128), F32),
-            pltpu.VMEM((2, CH, 2 * FCH, LAG), BF16),
             dma((9,)), dma((3, NCH)), dma((3, NCH)), dma, dma((4, NCH)), dma((4, NCH)),
             dma((NCH,)), dma((NCH,)), dma((NCH,)), dma((NCH,)),
-            dma((NCH,)), dma((NCH,)), dma((2,)),
+            dma((NCH,)), dma((NCH,)),
         ],
         compiler_params=pltpu.CompilerParams(
-            collective_id=0, has_side_effects=True, vmem_limit_bytes=48 << 20),
+            collective_id=0, has_side_effects=True, vmem_limit_bytes=58 << 20),
     )(traces, table)
     part = 16
     return pl.pallas_call(

time: 102 us -> 99.9 us (0.979)
  local copies, waits for them, and re-layouts: 2.63 us -> 0 us
    unnamed x4 -> x0, local copies, waits for them, and re-layouts: 2.63 us -> none
where the time goes in v4:
time: 99.9 us; the launch traced here: 99.6 us
  Pallas kernels  99.6 us (100%)
    pallas_call x1, Pallas kernels, per_device(): pl.pallas_call(stack_kernel, out_shape=jax.ShapeDtypeStruct((NCH, CH, 2 *...  93.7 us
    pallas_call x1, Pallas kernels, per_device(): pl.pallas_call(widen_kernel, grid=(CH // part,), out_shape=jax.ShapeDtype...  5.96 us

profile of v4, /device:TPU:1, one launch (start us, length us, event | category | flops | bytes accessed | tf_op | source)
XLA Modules:
  0.0 99.6 jit_solution(16880457058052535911)
XLA Ops:
  0.0 93.7 %shard_map.28.in_ref = bf16[8,64,16,256]{3,2,1,0:T(8,128)(2,1)} custom-call(bf16[64,32,512]{2,1,0:T(8,128)(2,1)} %tr_hbm.1, bf16[512,512]{1,0:T(8,128)(2,1)} %constant.2.clone.kt_hbm), custom_call_target="tpu_custom_call" | custom-call | tf_op jit(solution)/shard_map/pallas_call | solution.py:479
  93.7 6.0 %shard_map.29 = f32[64,2,64,256]{3,2,1,0:T(8,128)} custom-call(bf16[8,64,16,256]{3,2,1,0:T(8,128)(2,1)} %shard_map.28.in_ref), custom_call_target="tpu_custom_call" | custom-call | tf_op jit(solution)/shard_map/pallas_call | solution.py:504

commit v5 on v4

--- a/solution.py
+++ b/solution.py
@@ -24,7 +24,7 @@
 DEPTH = 2 * WIN * SEG
 ROWY = 4
 SCALE = 1.0 / math.sqrt(WIN * SEG)
-FETCHED = ((), (2, 5), (2, 5), (3,))
+FETCHED = ((4,), (1, 4), (1, 4), (2,))
 FETCHED_FAR = ((), (2, 4, 6), (2, 4, 6), (2,5))
 FETCHED_NEAR = (0,1,3,5,7)
 AHEAD = 2

time: 99.9 us -> 99.9 us (level)
  no operation moved by 1% of the time
where the time goes in v5:
time: 99.9 us; the launch traced here: 99.6 us
  Pallas kernels  99.6 us (100%)
    pallas_call x1, Pallas kernels, per_device(): pl.pallas_call(stack_kernel, out_shape=jax.ShapeDtypeStruct((NCH, CH, 2 *...  93.7 us
    pallas_call x1, Pallas kernels, per_device(): pl.pallas_call(widen_kernel, grid=(CH // part,), out_shape=jax.ShapeDtype...  5.96 us

profile of v5, /device:TPU:1, one launch (start us, length us, event | category | flops | bytes accessed | tf_op | source)
XLA Modules:
  0.0 99.6 jit_solution(10822416635138571577)
XLA Ops:
  0.0 93.7 %shard_map.28.in_ref = bf16[8,64,16,256]{3,2,1,0:T(8,128)(2,1)} custom-call(bf16[64,32,512]{2,1,0:T(8,128)(2,1)} %tr_hbm.1, bf16[512,512]{1,0:T(8,128)(2,1)} %constant.2.clone.kt_hbm), custom_call_target="tpu_custom_call" | custom-call | tf_op jit(solution)/shard_map/pallas_call | solution.py:479
  93.7 6.0 %shard_map.29 = f32[64,2,64,256]{3,2,1,0:T(8,128)} custom-call(bf16[8,64,16,256]{3,2,1,0:T(8,128)(2,1)} %shard_map.28.in_ref), custom_call_target="tpu_custom_call" | custom-call | tf_op jit(solution)/shard_map/pallas_call | solution.py:504
